TPU v7x, 32 devices: a whole 2x2x4 slice. The times are simulated.
32 devices in a mesh: groups: 2 (over y), freq: 4 (over z), src: 2 (over x), vp: 2 (over core).
Axes of the slice: x: 2, y: 2, z: 4, core: 2. Of those that a mesh axis runs over, the one named last changes fastest.
Arguments:
- focus_direct: bfloat16 [4, 2, 192, 8192], P('freq', None, ('groups', 'vp'), 'src'), parts along dimension 2, may hold values from -6 to 6
- u_factors: bfloat16 [4, 32, 2, 32, 2048], P('freq', 'src'), may hold values from -0.1875 to 0.1875
- v_factors: bfloat16 [4, 8, 2, 32, 8192], P('freq', None, None, None, 'src'), may hold values from -0.375 to 0.375
- tile_ranks: int32 [4, 8, 32], P('freq', None, 'src'), may hold values from 16 to 32
- onset_rec: int32 [192, 2048], P(('groups', 'vp'), 'src'), parts along dimension 0, may hold values from 64 to 191
- onset_src: int32 [192, 8192], P(('groups', 'vp'), 'src'), parts along dimension 0, may hold values from 64 to 191
Outputs:
- focus_plus: bfloat16 [4, 2, 192, 8192], P('freq', None, ('groups', 'vp'), 'src'), parts along dimension 2
- focus_minus: bfloat16 [4, 2, 192, 2048], P('freq', None, ('groups', 'vp'), 'src'), parts along dimension 2
There are 2 independent parts, one for each index of `groups`. A program takes and returns all parts, laid end to end along the dimension named above; an argument that names none is the same for every part. Nothing has to cross between parts.
All inputs are finite; a program needn't handle non-finite values.
Results may differ from a plain program's by a relative error of at most 0.018.
Values may be sent and summed in bfloat16 or wider, within the bound.
A program may use at most 128 MiB of HBM per device.

v0:
```python
import math

import jax
import jax.numpy as jnp
from jax import lax
from jax.sharding import PartitionSpec as P

TILE = 256
RANK = 32
NT = 256
FLO = 8
ITERS = 2


def make_tables(count):
    index = FLO + jnp.arange(count, dtype=jnp.int32)
    sample = jnp.arange(NT, dtype=jnp.int32)
    phase = (index[:, None] * sample[None, :] % NT).astype(jnp.float32) * (2.0 * math.pi / NT)
    cosine = jnp.cos(phase)
    sine = jnp.sin(phase)
    inverse = jnp.stack([cosine, -sine]) * (2.0 / NT)
    forward = jnp.stack([cosine, -sine])
    return (inverse, forward)


def window(spectrum, onset):
    inverse, forward = make_tables(spectrum.shape[0])
    signal = jnp.einsum("fcvm,cft->vmt", spectrum, inverse, precision=lax.Precision.HIGHEST)
    keep = jnp.arange(NT, dtype=jnp.int32)[None, None, :] < onset[:, :, None]
    signal = jnp.where(keep, signal, jnp.zeros_like(signal))
    return jnp.einsum("vmt,cft->fcvm", signal, forward, precision=lax.Precision.HIGHEST)


def coefficients(v_fac, mask, focus):
    points = focus.shape[1]
    row_tiles = v_fac.shape[0]
    col_tiles = v_fac.shape[-1] // TILE
    source = focus.reshape(2, points, col_tiles, TILE)
    v_tiles = v_fac.reshape(row_tiles, 2, RANK, col_tiles, TILE)
    form = "irjt,vjt->ivjr"
    z_real = jnp.einsum(
        form, v_tiles[:, 0], source[0], preferred_element_type=jnp.float32
    ) + jnp.einsum(form, v_tiles[:, 1], source[1], preferred_element_type=jnp.float32)
    z_imag = jnp.einsum(
        form, v_tiles[:, 0], source[1], preferred_element_type=jnp.float32
    ) - jnp.einsum(form, v_tiles[:, 1], source[0], preferred_element_type=jnp.float32)
    z_real = jnp.where(mask, z_real, 0.0).astype(jnp.bfloat16)
    z_imag = jnp.where(mask, z_imag, 0.0).astype(jnp.bfloat16)
    return jnp.stack([z_real, z_imag])


def expand_rows(u_fac, coeff):
    col_tiles = u_fac.shape[0]
    row_tiles = u_fac.shape[-1] // TILE
    points = coeff.shape[2]
    u_tiles = u_fac.reshape(col_tiles, 2, RANK, row_tiles, TILE)
    other = "jrit,ivjr->vit"
    y_real = jnp.einsum(
        other, u_tiles[:, 0], coeff[0], preferred_element_type=jnp.float32
    ) - jnp.einsum(other, u_tiles[:, 1], coeff[1], preferred_element_type=jnp.float32)
    y_imag = jnp.einsum(
        other, u_tiles[:, 0], coeff[1], preferred_element_type=jnp.float32
    ) + jnp.einsum(other, u_tiles[:, 1], coeff[0], preferred_element_type=jnp.float32)
    return jnp.stack([y_real.reshape(points, -1), y_imag.reshape(points, -1)])


def forward_local(u_fac, v_fac, mask, focus):
    return expand_rows(u_fac, coefficients(v_fac, mask, focus))


def adjoint_local(u_fac, v_fac, mask, focus):
    points = focus.shape[1]
    col_tiles = u_fac.shape[0]
    row_tiles = v_fac.shape[0]
    receiver = focus.reshape(2, points, row_tiles, TILE)
    v_tiles = v_fac.reshape(row_tiles, 2, RANK, col_tiles, TILE)
    u_tiles = u_fac.reshape(col_tiles, 2, RANK, row_tiles, TILE)
    form = "jrit,vit->ivjr"
    w_real = jnp.einsum(
        form, u_tiles[:, 0], receiver[0], preferred_element_type=jnp.float32
    ) + jnp.einsum(form, u_tiles[:, 1], receiver[1], preferred_element_type=jnp.float32)
    w_imag = jnp.einsum(
        form, u_tiles[:, 0], receiver[1], preferred_element_type=jnp.float32
    ) - jnp.einsum(form, u_tiles[:, 1], receiver[0], preferred_element_type=jnp.float32)
    w_real = jnp.where(mask, w_real, 0.0).astype(jnp.bfloat16)
    w_imag = jnp.where(mask, w_imag, 0.0).astype(jnp.bfloat16)
    other = "irjt,ivjr->vjt"
    x_real = jnp.einsum(
        other, v_tiles[:, 0], w_real, preferred_element_type=jnp.float32
    ) - jnp.einsum(other, v_tiles[:, 1], w_imag, preferred_element_type=jnp.float32)
    x_imag = jnp.einsum(
        other, v_tiles[:, 0], w_imag, preferred_element_type=jnp.float32
    ) + jnp.einsum(other, v_tiles[:, 1], w_real, preferred_element_type=jnp.float32)
    return jnp.stack([x_real.reshape(points, -1), x_imag.reshape(points, -1)])


def per_device(focus_direct, u_factors, v_factors, tile_ranks, onset_rec, onset_src):
    freq_count = lax.axis_size("freq")
    rank_index = jnp.arange(RANK, dtype=jnp.int32)
    masks = (rank_index[None, None, None, :] < tile_ranks[:, :, :, None])[:, :, None]
    rec_block = onset_rec.shape[1]
    rec_piece = rec_block // freq_count
    src_piece = onset_src.shape[1] // freq_count
    freq_place = lax.axis_index("freq")
    rec_onset = lax.dynamic_slice_in_dim(onset_rec, freq_place * rec_piece, rec_piece, 1)
    src_onset = lax.dynamic_slice_in_dim(onset_src, freq_place * src_piece, src_piece, 1)
    plus = focus_direct
    minus = None
    for sweep in range(ITERS):
        partial_terms = jax.vmap(forward_local)(u_factors, v_factors, masks, plus)
        summed = lax.psum_scatter(
            partial_terms.astype(jnp.bfloat16), "src", scatter_dimension=3, tiled=True
        ).astype(jnp.float32)
        traces = lax.all_to_all(
            summed.astype(jnp.bfloat16), "freq", split_axis=3, concat_axis=0, tiled=True
        ).astype(summed.dtype)
        windowed = window(traces, rec_onset).astype(jnp.bfloat16)
        minus = lax.all_to_all(windowed, "freq", split_axis=0, concat_axis=3, tiled=True)
        minus_all = lax.all_gather(minus, "src", axis=3, tiled=True)
        adjoint = jax.vmap(adjoint_local)(u_factors, v_factors, masks, minus_all)
        source_traces = lax.all_to_all(
            adjoint.astype(jnp.bfloat16), "freq", split_axis=3, concat_axis=0, tiled=True
        ).astype(adjoint.dtype)
        src_windowed = window(source_traces, src_onset)
        returned = lax.all_to_all(
            src_windowed.astype(jnp.bfloat16), "freq", split_axis=0, concat_axis=3, tiled=True
        ).astype(src_windowed.dtype)
        plus = (focus_direct.astype(jnp.float32) + returned).astype(jnp.bfloat16)
    return (plus, minus)


def solution(mesh):
    placed = (
        P("freq", None, ("groups", "vp"), "src"),
        P("freq", "src", None, None, None),
        P("freq", None, None, None, "src"),
        P("freq", None, "src"),
        P(("groups", "vp"), "src"),
        P(("groups", "vp"), "src"),
    )
    return jax.shard_map(
        per_device,
        mesh=mesh,
        in_specs=placed,
        out_specs=(
            P("freq", None, ("groups", "vp"), "src"),
            P("freq", None, ("groups", "vp"), "src"),
        ),
        check_vma=False,
    )
```

profile of v0, /device:TPU:0, one launch (start us, length us, event | category | flops | bytes accessed | tf_op | source)
XLA Modules:
  0.0 478.2 jit_solution(13236355608998709984)
XLA Ops:
  7.2 1.4 copy.194
  8.7 3.6 copy.195
  12.3 3.3 slice_bitcast_fusion.2
  16.3 2.1 fusion.160
  18.4 2.1 fusion.159
  21.2 2.1 fusion.158
  23.3 2.1 fusion.161
  25.5 3.7 copy.196
  29.2 3.2 slice_bitcast_fusion
  32.4 1.6 copy-done.18
  34.9 1.4 fusion.151
  41.8 15.2 %reduce-scatter.3.cloned.1.call-done = bf16[1,2,48,1024]{3,2,1,0:T(8,128)(2,1)} async-done(((bf16[1,2,48,2048]{3,2,1,0:T(8,128)(2,1)}), bf16[1,2,48,1024]{3,2,1,0:T(8,128)(2,1)}) %reduce-scatter.3.cloned.1.call-update) | async-done | bytes 196624 | tf_op jit(solution)/shard_map/reduce_scatter | solution.py:111
  58.2 1.5 reshape.568
  59.7 4.6 all-to-all-start
  64.4 7.4 %all-to-all-done = bf16[4,2,12288]{2,1,0:T(2,128)(2,1)} async-done(((bf16[4,2,12288]{2,1,0:T(2,128)(2,1)}), bf16[4,2,12288]{2,1,0:T(2,128)(2,1)}, u32[]{:S(2)}, u32[]{:S(2)}) %all-to-all-start) | async-done | bytes 196640 | tf_op jit(solution)/shard_map/all_to_all | solution.py:114
  71.8 1.4 reshape.569
  74.3 6.0 %fusion.168 = f32[48,256,256,1]{2,1,0,3:T(8,128)S(1)} fusion(bf16[1,2,48,4,256]{4,3,2,1,0:T(4,128)(2,1)} %copy.170, f32[1,4,256]{2,1,0:T(4,128)S(1)} %get-tuple-element.27, f32[1,4,256]{2,1,0:T(4,128)S(1)} %get-tuple-element.26), kind=kOutput, calls=%fused_computation.144 | convolution fusion | flops 301993984 | bytes 12787712 | tf_op jit(solution)/shard_map/fcvm,cft->vmt/dot_general | solution.py:28
  80.3 12.0 %fusion.143 = bf16[4,2,48,256]{3,0,2,1:T(4,128)(2,1)S(1)} fusion(f32[48,256,256,1]{2,1,0,3:T(8,128)S(1)} %fusion.168, s32[48,256]{1,0:T(8,128)S(1)} %constant_dynamic-slice_fusion, f32[1,4,256]{2,1,0:T(4,128)S(1)} %get-tuple-element.27, f32[1,4,256]{2,1,0:T(4,128)S(1)} %get-tuple-element.26), kind=kOutput, calls=%fused_computation.109 | convolution fusion | flops 308381696 | bytes 12836864 | tf_op jit(solution)/shard_map/vmt,cft->fcvm/dot_general | solution.py:31
  93.1 3.6 all-to-all-start.1
  96.7 3.6 copy.131
  100.3 1.9 copy.129
  102.9 6.5 %all_gather.6 = bf16[1,2,48,2048]{3,2,1,0:T(8,128)(2,1)S(1)} all-gather(bf16[1,2,48,1024]{3,2,1,0:T(8,128)(2,1)S(1)} %bitcast.606), channel_id=1, replica_groups=mesh['groups'=2,'freq'=4,'src'=2,'vp'=2] {'src'}, dimensions={3}, use_global_device_ids=true | all-gather | bytes 589824 | tf_op jit(solution)/shard_map/all_gather | solution.py:119
  119.7 1.9 reshape.493
  123.7 1.9 maximum_bitcast_fusion
  125.6 5.4 %copy.140 = bf16[1,2,48,4096]{2,1,0,3:T(2,128)(2,1)} copy(bf16[1,2,48,4096]{3,2,1,0:T(8,128)(2,1)} %maximum_bitcast_fusion) | data formatting | bytes 1572864 | tf_op jit(solution)/shard_map/convert_element_type | solution.py:122
  131.1 5.1 %reshape.570 = bf16[4,2,49152]{2,1,0:T(2,128)(2,1)} reshape(bf16[4096,1,2,48]{3,2,1,0:T(2,128)(2,1)} %bitcast.582) | data formatting | bytes 1572864
  136.2 4.3 all-to-all-start.2
  140.6 17.3 %all-to-all-done.2 = bf16[4,2,49152]{2,1,0:T(2,128)(2,1)} async-done(((bf16[4,2,49152]{2,1,0:T(2,128)(2,1)}), bf16[4,2,49152]{2,1,0:T(2,128)(2,1)}, u32[]{:S(2)}, u32[]{:S(2)}) %all-to-all-start.2) | async-done | bytes 786464 | tf_op jit(solution)/shard_map/all_to_all | solution.py:121
  157.9 4.9 %reshape.571 = bf16[4096,1,2,48]{3,2,1,0:T(2,128)(2,1)} reshape(bf16[4,2,49152]{2,1,0:T(2,128)(2,1)} %all-to-all-done.2) | data formatting | bytes 1572864
  162.8 5.0 %copy.171 = bf16[1,2,48,4,1024]{4,3,2,1,0:T(4,128)(2,1)S(1)} copy(bf16[1,2,48,4,1024]{2,1,4,3,0:T(2,128)(2,1)} %bitcast.583) | data formatting | bytes 1572864 | tf_op jit(solution)/shard_map/all_to_all | solution.py:121
  167.8 24.2 %fusion.156 = f32[48,1024,256,1]{2,1,0,3:T(8,128)} fusion(bf16[1,2,48,4,1024]{4,3,2,1,0:T(4,128)(2,1)S(1)} %copy.171, f32[1,4,256]{2,1,0:T(4,128)S(1)} %get-tuple-element.27, f32[1,4,256]{2,1,0:T(4,128)S(1)} %get-tuple-element.26), kind=kOutput, calls=%fused_computation.122 | convolution fusion | flops 1207963648 | bytes 51126272 | tf_op jit(solution)/shard_map/fcvm,cft->vmt/dot_general | solution.py:28
  192.1 46.6 %fusion.79 = bf16[4,2,48,1024]{3,0,2,1:T(4,128)(2,1)S(1)} fusion(f32[48,1024,256,1]{2,1,0,3:T(8,128)} %fusion.156, s32[48,1024]{1,0:T(8,128)S(1)} %constant_dynamic-slice_fusion.1, f32[1,4,256]{2,1,0:T(4,128)S(1)} %get-tuple-element.27, f32[1,4,256]{2,1,0:T(4,128)S(1)} %get-tuple-element.26), kind=kOutput, calls=%fused_computation.77 | convolution fusion | flops 1233520640 | bytes 51322880 | tf_op jit(solution)/shard_map/vmt,cft->fcvm/dot_general | solution.py:31
  238.9 20.7 %all_to_all.126 = bf16[4,2,48,1024]{3,2,1,0:T(8,128)(2,1)S(1)} all-to-all(bf16[4,2,48,1024]{3,2,1,0:T(8,128)(2,1)S(1)} %copy.142), channel_id=1, replica_groups=mesh['groups'=2,'freq'=4,'src'=2,'vp'=2] {'freq'}, dimensions={0} | all-to-all | bytes 1572864 | tf_op jit(solution)/shard_map/all_to_all | solution.py:125
  272.6 11.4 %reduce-scatter.5.cloned.1.call-done = bf16[1,2,48,1024]{3,2,1,0:T(8,128)(2,1)} async-done(((bf16[1,2,48,2048]{3,2,1,0:T(8,128)(2,1)}), bf16[1,2,48,1024]{3,2,1,0:T(8,128)(2,1)}) %reduce-scatter.5.cloned.1.call-update) | async-done | bytes 196624 | tf_op jit(solution)/shard_map/reduce_scatter | solution.py:111
  286.0 12.1 %all_to_all.127 = bf16[4,2,12288]{2,1,0:T(2,128)(2,1)S(1)} all-to-all(bf16[4,2,12288]{2,1,0:T(2,128)(2,1)S(1)} %reshape.572), channel_id=1, replica_groups=mesh['groups'=2,'freq'=4,'src'=2,'vp'=2] {'freq'}, dimensions={0} | all-to-all | bytes 393216 | tf_op jit(solution)/shard_map/all_to_all | solution.py:114
  299.1 5.1 %fusion.166 = f32[48,256,256,1]{2,1,0,3:T(8,128)S(1)} fusion(bf16[1,2,48,4,256]{4,3,2,1,0:T(4,128)(2,1)S(1)} %copy.172, f32[1,4,256]{2,1,0:T(4,128)S(1)} %get-tuple-element.27, f32[1,4,256]{2,1,0:T(4,128)S(1)} %get-tuple-element.26), kind=kOutput, calls=%fused_computation.142 | convolution fusion | flops 301993984 | bytes 12787712 | tf_op jit(solution)/shard_map/fcvm,cft->vmt/dot_general | solution.py:28
  304.2 12.0 %fusion.140 = bf16[4,2,48,256]{3,0,2,1:T(4,128)(2,1)S(1)} fusion(f32[48,256,256,1]{2,1,0,3:T(8,128)S(1)} %fusion.166, s32[48,256]{1,0:T(8,128)S(1)} %constant_dynamic-slice_fusion, f32[1,4,256]{2,1,0:T(4,128)S(1)} %get-tuple-element.27, f32[1,4,256]{2,1,0:T(4,128)S(1)} %get-tuple-element.26), kind=kOutput, calls=%fused_computation.108 | convolution fusion | flops 308381696 | bytes 12836864 | tf_op jit(solution)/shard_map/vmt,cft->fcvm/dot_general | solution.py:31
  316.3 10.0 %all_to_all.128 = bf16[4,2,48,256]{3,2,1,0:T(8,128)(2,1)S(1)} all-to-all(bf16[4,2,48,256]{3,2,1,0:T(8,128)(2,1)S(1)} %copy.150), channel_id=1, replica_groups=mesh['groups'=2,'freq'=4,'src'=2,'vp'=2] {'freq'}, dimensions={0} | all-to-all | bytes 393216 | tf_op jit(solution)/shard_map/all_to_all | solution.py:118
  326.3 6.3 %all_gather.7 = bf16[1,2,48,2048]{3,2,1,0:T(8,128)(2,1)S(1)} all-gather(bf16[1,2,48,1024]{3,2,1,0:T(8,128)(2,1)S(1)} %bitcast.604), channel_id=1, replica_groups=mesh['groups'=2,'freq'=4,'src'=2,'vp'=2] {'src'}, dimensions={3}, use_global_device_ids=true | all-gather | bytes 589824 | tf_op jit(solution)/shard_map/all_gather | solution.py:119
  336.5 1.5 select_convert_fusion.1
  342.9 2.8 copy.164
  345.7 3.3 reshape.574
  349.0 21.8 %all_to_all.129 = bf16[4,2,49152]{2,1,0:T(2,128)(2,1)} all-to-all(bf16[4,2,49152]{2,1,0:T(2,128)(2,1)S(1)} %reshape.574), channel_id=1, replica_groups=mesh['groups'=2,'freq'=4,'src'=2,'vp'=2] {'freq'}, dimensions={0} | all-to-all | bytes 1572864 | tf_op jit(solution)/shard_map/all_to_all | solution.py:121
  370.8 3.4 reshape.575
  374.3 1.6 copy.173
  375.9 24.2 %fusion.154 = f32[48,1024,256,1]{2,1,0,3:T(8,128)} fusion(bf16[1,2,48,4,1024]{4,3,2,1,0:T(4,128)(2,1)S(1)} %copy.173, f32[1,4,256]{2,1,0:T(4,128)S(1)} %get-tuple-element.27, f32[1,4,256]{2,1,0:T(4,128)S(1)} %get-tuple-element.26), kind=kOutput, calls=%fused_computation.120 | convolution fusion | flops 1207963648 | bytes 51126272 | tf_op jit(solution)/shard_map/fcvm,cft->vmt/dot_general | solution.py:28
  400.1 46.6 %fusion.76 = bf16[4,2,48,1024]{3,0,2,1:T(4,128)(2,1)S(1)} fusion(f32[48,1024,256,1]{2,1,0,3:T(8,128)} %fusion.154, s32[48,1024]{1,0:T(8,128)S(1)} %constant_dynamic-slice_fusion.1, f32[1,4,256]{2,1,0:T(4,128)S(1)} %get-tuple-element.27, f32[1,4,256]{2,1,0:T(4,128)S(1)} %get-tuple-element.26), kind=kOutput, calls=%fused_computation.76 | convolution fusion | flops 1233520640 | bytes 51322880 | tf_op jit(solution)/shard_map/vmt,cft->fcvm/dot_general | solution.py:31
  447.0 21.5 %all_to_all.130 = bf16[4,2,48,1024]{3,2,1,0:T(8,128)(2,1)S(1)} all-to-all(bf16[4,2,48,1024]{3,2,1,0:T(8,128)(2,1)S(1)} %copy.166), channel_id=1, replica_groups=mesh['groups'=2,'freq'=4,'src'=2,'vp'=2] {'freq'}, dimensions={0} | all-to-all | bytes 1572864 | tf_op jit(solution)/shard_map/all_to_all | solution.py:125
  (136 shorter events, 51.5 us)
Async XLA Ops:
  7.2 133.4 %copy-start = (s32[48,4096]{1,0:T(8,128)S(1)}, s32[48,4096]{1,0:T(8,128)}, u32[]{:S(2)}) copy-start(s32[48,4096]{1,0:T(8,128)} %param.11) | copy-start | bytes 2359300
  7.2 49.7 %reduce-scatter.3.cloned.1.call-start = ((), (), s32[]{:S(2)}) async-start(), calls=%async_computation.10 | async-start | bytes 589824 | tf_op jit(solution)/shard_map/reduce_scatter | solution.py:111
  16.3 2.1 copy-start.2
  21.2 2.1 copy-start.4
  23.3 2.1 copy-start.24
  29.2 3.2 copy-start.16
  29.2 3.2 copy-start.17
  29.2 4.8 copy-start.18
  29.2 5.7 %copy-start.19 = (f32[16,48,256]{1,2,0:S(1)}, f32[16,48,256]{1,2,0}, u32[]{:S(2)}) copy-start(f32[16,48,256]{1,2,0} %fusion.161) | copy-start | bytes 2359300
  32.4 4.8 %copy-start.6 = (bf16[1,16,1,32,8,256]{5,4,3,2,1,0:T(8,128)(2,1)}, bf16[1,16,1,32,8,256]{5,4,3,2,1,0:T(8,128)(2,1)S(1)}, u32[]{:S(2)}) copy-start(bf16[1,16,1,32,8,256]{5,4,3,2,1,0:T(8,128)(2,1)S(1)} %get-tuple-element.9) | copy-start | bytes 6291460
  59.7 12.2 %all-to-all-start = ((bf16[4,2,12288]{2,1,0:T(2,128)(2,1)}), bf16[4,2,12288]{2,1,0:T(2,128)(2,1)}, u32[]{:S(2)}, u32[]{:S(2)}) async-start(bf16[4,2,12288]{2,1,0:T(2,128)(2,1)} %reshape.568), calls=%async_computation.1 | async-start | bytes 393216 | tf_op jit(solution)/shard_map/all_to_all | solution.py:114
  93.1 9.8 %all-to-all-start.1 = ((bf16[4,2,48,256]{3,2,1,0:T(8,128)(2,1)}), bf16[4,2,48,256]{3,2,1,0:T(8,128)(2,1)S(1)}, u32[]{:S(2)}, u32[]{:S(2)}) async-start(bf16[4,2,48,256]{3,2,1,0:T(8,128)(2,1)} %copy.126), calls=%async_computation.2 | async-start | bytes 393216 | tf_op jit(solution)/shard_map/all_to_all | solution.py:118
  96.7 3.6 copy-start.20
  102.9 6.6 %copy-start.8 = (bf16[16,32,8,256]{3,1,0,2:T(8,128)(2,1)S(1)}, bf16[16,32,8,256]{3,1,0,2:T(8,128)(2,1)}, u32[]{:S(2)}) copy-start(bf16[16,32,8,256]{3,1,0,2:T(8,128)(2,1)} %copy.131) | copy-start | bytes 6291460
  109.5 1.6 copy-start.10
  113.2 1.6 copy-start.14
  115.6 1.6 copy-start.12
  136.2 21.7 %all-to-all-start.2 = ((bf16[4,2,49152]{2,1,0:T(2,128)(2,1)}), bf16[4,2,49152]{2,1,0:T(2,128)(2,1)}, u32[]{:S(2)}, u32[]{:S(2)}) async-start(bf16[4,2,49152]{2,1,0:T(2,128)(2,1)} %reshape.570), calls=%async_computation.3 | async-start | bytes 1572864 | tf_op jit(solution)/shard_map/all_to_all | solution.py:121
  140.6 143.4 %reduce-scatter.5.cloned.1.call-start = ((), (), s32[]{:S(2)}) async-start(), calls=%async_computation.11 | async-start | bytes 589824 | tf_op jit(solution)/shard_map/reduce_scatter | solution.py:111
  259.8 1.1 copy-start.21
  261.1 1.6 copy-start.3
  262.7 1.6 copy-start.5
  266.4 1.6 copy-start.7
  316.2 16.6 %copy-start.9 = (bf16[16,32,8,256]{3,1,0,2:T(8,128)(2,1)S(1)}, bf16[16,32,8,256]{3,1,0,2:T(8,128)(2,1)}, u32[]{:S(2)}) copy-start(bf16[16,32,8,256]{3,1,0,2:T(8,128)(2,1)} %copy.131) | copy-start | bytes 6291460
  326.3 6.4 %copy-start.23 = (bf16[1,4,2,6,8,256]{5,4,1,3,2,0:T(8,128)(2,1)}, bf16[1,4,2,6,8,256]{5,4,1,3,2,0:T(8,128)(2,1)S(1)}, u32[]{:S(2)}) copy-start(bf16[1,4,2,6,8,256]{5,4,1,3,2,0:T(8,128)(2,1)S(1)} %copy.192) | copy-start | bytes 589828
  332.8 1.6 copy-start.11
  336.5 1.6 copy-start.15
  338.9 1.6 copy-start.13
  468.7 1.1 copy-start.22
  468.7 2.2 copy-start.1
Sparse Core Ops, SparseCore 0:
  41.1 15.7 reduce-scatter.2
  272.7 11.1 reduce-scatter.4
where the time goes:
time: 486 us; the launch traced here: 478 us
  matrix products  207 us (43%)
  blocking collectives  99 us (20%)
  local copies, waits for them, and re-layouts  81.7 us (17%)
  waiting for transfers between devices  52 us (11%)
  between operations  15.2 us (3%)
  starting transfers between devices  12.6 us (3%)
  other arithmetic  10.8 us (2%)
    dot_general x4, matrix products, window(): jnp.einsum('vmt,cft->fcvm', signal, forward, precision=lax.Precision.HIGH...  117 us
    dot_general x4, matrix products, window(): jnp.einsum('fcvm,cft->vmt', spectrum, inverse, precision=lax.Precision.HI...  59.6 us
    unnamed x66, local copies, waits for them, and re-layouts  42.3 us
    all_to_all x2, blocking collectives, per_device(): lax.all_to_all(src_windowed.astype(jnp.bfloat16), 'freq', split_axis=0, c...  42.2 us
    reduce_scatter x2, waiting for transfers between devices, per_device(): lax.psum_scatter(partial_terms.astype(jnp.bfloat16), 'src', scatter_dimen...  26.5 us
    all_to_all x1, blocking collectives, per_device(): lax.all_to_all(adjoint.astype(jnp.bfloat16), 'freq', split_axis=3, concat...  21.8 us
    all_to_all x1, waiting for transfers between devices, per_device(): lax.all_to_all(adjoint.astype(jnp.bfloat16), 'freq', split_axis=3, concat...  17.3 us
    unnamed x16, matrix products  16.6 us
  transfers between devices with their start and end apart: 5, of which 5 were waited for; matrix products, arithmetic and copies ran while one was open for 1% of the time, Pallas kernels for 0%

commit v1 on v0

--- a/solution.py
+++ b/solution.py
@@ -1,8 +1,12 @@
+import cmath
+import functools
 import math
 
 import jax
 import jax.numpy as jnp
 from jax import lax
+from jax.experimental import pallas as pl
+from jax.experimental.pallas import tpu as pltpu
 from jax.sharding import PartitionSpec as P
 
 TILE = 256
@@ -10,6 +14,8 @@
 NT = 256
 FLO = 8
 ITERS = 2
+CHUNK = 16
+LANES = 128
 
 
 def make_tables(count):
@@ -129,6 +135,431 @@
     return (plus, minus)
 
 
+def lane_index(rows):
+    return lax.broadcasted_iota(jnp.int32, (rows, LANES), 1)
+
+
+def combine(x):
+    half = x.shape[0] // 2
+    lane = lane_index(x.shape[0])
+    row = lax.broadcasted_iota(jnp.int32, x.shape, 0)
+    first = (lane % (2 * RANK)) < RANK
+    other = jnp.concatenate([x[half:], x[:half]], axis=0)
+    moved = jnp.where(first, pltpu.roll(other, LANES - RANK, 1), pltpu.roll(other, RANK, 1))
+    return jnp.where(first == (row < half), x + moved, x - moved)
+
+
+def pair_up(a, b):
+    low = lane_index(a.shape[0]) < 2 * RANK
+    return (
+        jnp.where(low, a, pltpu.roll(b, 2 * RANK, 1)),
+        jnp.where(low, pltpu.roll(a, 2 * RANK, 1), b),
+    )
+
+
+def masked(x, rank_a, rank_b):
+    lane = lane_index(x.shape[0])
+    rank = jnp.where(lane < 2 * RANK, rank_a, rank_b)
+    return jnp.where(lane % RANK < rank, x, 0.0).astype(jnp.bfloat16)
+
+
+def times(a, b):
+    return (a[0] * b[0] - a[1] * b[1], a[0] * b[1] + a[1] * b[0])
+
+
+def window_terms(onset, count):
+    samples = onset.astype(jnp.float32)
+    angle = (samples - NT / 2) * (math.pi / NT)
+    square = angle * angle
+
+    def series(top):
+        total = jnp.full_like(square, 1.0)
+        for n in range(top, 1, -2):
+            total = 1.0 - square * total * (1.0 / (n * (n - 1)))
+        return total
+
+    sin_half = angle * series(13)
+    cos_half = series(14)
+    z = (sin_half * sin_half - cos_half * cos_half, -2.0 * sin_half * cos_half)
+    powers = {1: z}
+
+    def power(m):
+        if m not in powers:
+            low = m // 2 if m % 2 == 0 else m - 1
+            powers[m] = times(power(low), power(m - low))
+        return powers[m]
+
+    def term(m):
+        if m == 0:
+            return (samples * (1.0 / NT), None)
+        scale = 1.0 / (cmath.exp(2j * math.pi * m / NT) - 1.0) / NT
+        re, im = power(m)
+        re = re - 1.0
+        return (re * scale.real - im * scale.imag, re * scale.imag + im * scale.real)
+
+    return [term(m) for m in range(count)], [term(m) for m in range(2 * FLO, 2 * (FLO + count) - 1)]
+
+
+def window_block(spectra, onset, count):
+    diff, total = window_terms(onset, count)
+    results = []
+    for out in range(count):
+        real = imag = None
+        for f in range(count):
+            x_re, x_im = spectra[f]
+            s_re, s_im = total[f + out]
+            d_re, d_im = diff[abs(f - out)]
+            if d_im is None:
+                a, b, c, d = d_re + s_re, -s_im, -s_im, d_re - s_re
+            else:
+                if f < out:
+                    d_im = -d_im
+                a, b, c, d = d_re + s_re, -(d_im + s_im), d_im - s_im, d_re - s_re
+            one, two = x_re * a + x_im * b, x_re * c + x_im * d
+            real = one if real is None else real + one
+            imag = two if imag is None else imag + two
+        results.append((real, imag))
+    return results
+
+
+NT_DOT = (((1,), (1,)), ((), ()))
+
+
+def kernel(
+    axes, focus_hbm, u_hbm, v_hbm, ranks, onset_rec_hbm, onset_src_hbm, plus_hbm, minus_hbm,
+    focus, u_fac, v_fac, onset_rec, onset_src, plus, coeff, back, kept,
+    x_out, x_in, a_out, a_in, b_out, b_in, d_in, g_out, g_in, h_out, h_in,
+    load_sem, store_sem, x_sems, d_sems, a_sems, b_sems, g_sems, h_sems,
+):
+    freqs, sides = axes["freq"], axes["src"]
+    here = lax.axis_index("freq")
+    side = lax.axis_index("src")
+    partner = 1 - side
+    points = focus.shape[1]
+    chunks = points // CHUNK
+    row_tiles = u_fac.shape[1] // TILE
+    col_tiles = v_fac.shape[1] // TILE
+    half = row_tiles // sides
+    rec_piece = onset_rec.shape[1]
+    src_piece = onset_src.shape[1]
+    tiles_each = src_piece // TILE
+
+    loads = [
+        pltpu.make_async_copy(focus_hbm, focus, load_sem.at[0]),
+        pltpu.make_async_copy(v_hbm, v_fac, load_sem.at[1]),
+        pltpu.make_async_copy(u_hbm, u_fac, load_sem.at[2]),
+        pltpu.make_async_copy(
+            onset_rec_hbm.at[:, pl.ds(pl.multiple_of(here * rec_piece, LANES), rec_piece)], onset_rec, load_sem.at[3]
+        ),
+        pltpu.make_async_copy(
+            onset_src_hbm.at[:, pl.ds(pl.multiple_of(here * src_piece, LANES), src_piece)], onset_src, load_sem.at[4]
+        ),
+    ]
+    for load in loads:
+        load.start()
+
+    barrier = pltpu.get_barrier_semaphore()
+    for step in range(1, freqs):
+        pl.semaphore_signal(
+            barrier, inc=1, device_id={"freq": lax.rem(here + step, freqs)}, device_id_type=pl.DeviceIdType.MESH
+        )
+    pl.semaphore_signal(barrier, inc=1, device_id={"src": partner}, device_id_type=pl.DeviceIdType.MESH)
+    pl.semaphore_wait(barrier, freqs)
+
+    sends = []
+    stores = []
+
+    def columns(index, size=TILE):
+        return pl.ds(pl.multiple_of(index * size, size), size)
+
+    def across(source, target, sems, k):
+        return pltpu.make_async_remote_copy(
+            src_ref=source, dst_ref=target, send_sem=sems.at[0, k], recv_sem=sems.at[1, k],
+            device_id={"src": partner}, device_id_type=pl.DeviceIdType.MESH,
+        )
+
+    def along(out, into, sems, k, step):
+        target = lax.rem(here + step, freqs)
+        return pltpu.make_async_remote_copy(
+            src_ref=out.at[k, target], dst_ref=into.at[k, here],
+            send_sem=sems.at[0, k, step - 1], recv_sem=sems.at[1, k, step - 1],
+            device_id={"freq": target}, device_id_type=pl.DeviceIdType.MESH,
+        )
+
+    def arrived(out, into, sems, k, step):
+        source = lax.rem(here + freqs - step, freqs)
+        pltpu.make_async_remote_copy(
+            src_ref=out.at[k, source], dst_ref=into.at[k, source],
+            send_sem=sems.at[0, k, step - 1], recv_sem=sems.at[1, k, step - 1],
+            device_id={"freq": source}, device_id_type=pl.DeviceIdType.MESH,
+        ).wait_recv()
+
+    def send(copy):
+        copy.start()
+        sends.append(copy)
+
+    def spread_out(first, second, into, store):
+        for q in range(first.shape[1] // LANES):
+            lanes = slice(q * LANES, (q + 1) * LANES)
+            even, odd = pair_up(combine(first[:, lanes]), combine(second[:, lanes]))
+            store(2 * q, even)
+            store(2 * q + 1, odd)
+
+    def forward(sweep, c):
+        k = sweep * chunks + c
+        rows = slice(c * CHUNK, (c + 1) * CHUNK)
+
+        def one(pair, carry):
+            products = []
+            for t in range(2):
+                cols = columns(2 * pair + t)
+                if sweep == 0:
+                    block = focus[:, rows, cols].reshape(2 * CHUNK, TILE)
+                else:
+                    block = plus[c, :, cols]
+                products.append(lax.dot_general(block, v_fac[:, cols], NT_DOT, preferred_element_type=jnp.float32))
+
+            def store(i, value):
+                coeff[i, :, columns(pair, LANES)] = masked(value, ranks[i, 2 * pair], ranks[i, 2 * pair + 1])
+
+            spread_out(products[0], products[1], coeff, store)
+            return carry
+
+        lax.fori_loop(0, col_tiles // 2, one, 0)
+        if sweep == 0 and c == 0:
+            loads[2].wait()
+
+        def product(i):
+            return jnp.dot(coeff[i], u_fac[:, columns(i)], preferred_element_type=jnp.float32)
+
+        def theirs(n, carry):
+            x_out[k, :, columns(n)] = product(partner * half + n).astype(jnp.bfloat16)
+            return carry
+
+        def ours(n, carry):
+            kept[c, :, columns(n)] = product(side * half + n)
+            return carry
+
+        lax.fori_loop(0, half, theirs, 0)
+        send(across(x_out.at[k], x_in.at[k], x_sems, k))
+        lax.fori_loop(0, half, ours, 0)
+
+    def reduce(sweep, c):
+        k = sweep * chunks + c
+        across(x_out.at[k], x_in.at[k], x_sems, k).wait_recv()
+        for q in range(freqs):
+            lanes = slice(q * rec_piece, (q + 1) * rec_piece)
+            a_out[k, q] = (kept[c, :, lanes] + x_in[k, :, lanes].astype(jnp.float32)).astype(jnp.bfloat16)
+        for step in range(1, freqs):
+            send(along(a_out, a_in, a_sems, k, step))
+        a_in[k, here] = a_out[k, here]
+
+    def window(k, c, from_ref, to_ref, own_ref, onset):
+        rows = slice(c * CHUNK, (c + 1) * CHUNK)
+
+        def one(n, carry):
+            lanes = columns(n, LANES)
+            spectra = []
+            for f in range(freqs):
+                both = from_ref[k, f, :, lanes].astype(jnp.float32)
+                spectra.append((both[:CHUNK], both[CHUNK:]))
+            for f, (real, imag) in enumerate(window_block(spectra, onset[rows, lanes], freqs)):
+                to_ref[k, f, :, lanes] = jnp.concatenate([real, imag], axis=0).astype(jnp.bfloat16)
+            return carry
+
+        lax.fori_loop(0, onset.shape[1] // LANES, one, 0)
+
+    def window_rec(sweep, c):
+        k = sweep * chunks + c
+        if sweep == 0 and c == 0:
+            loads[3].wait()
+        for step in range(1, freqs):
+            arrived(a_out, a_in, a_sems, k, step)
+        window(k, c, a_in, b_out, b_in, onset_rec)
+        for step in range(1, freqs):
+            send(along(b_out, b_in, b_sems, k, step))
+        b_in[k, here] = b_out[k, here]
+
+    def spread(sweep, c):
+        k = sweep * chunks + c
+        for step in range(1, freqs):
+            arrived(b_out, b_in, b_sems, k, step)
+        send(across(b_in.at[k], d_in.at[k], d_sems, k))
+        if sweep == ITERS - 1:
+            for part in range(2):
+                for q in range(freqs):
+                    store = pltpu.make_async_copy(
+                        b_in.at[k, q, pl.ds(part * CHUNK, CHUNK), :],
+                        minus_hbm.at[part, pl.ds(c * CHUNK, CHUNK), pl.ds(q * rec_piece, rec_piece)],
+                        store_sem.at[1, c, part * freqs + q],
+                    )
+                    store.start()
+                    stores.append(store)
+
+    def adjoint(sweep, c):
+        k = sweep * chunks + c
+
+        def back_pairs(source, first_tile):
+            def one(pair, carry):
+                products = []
+                for t in range(2):
+                    n = 2 * pair + t
+                    block = source[k, n * TILE // rec_piece, :, pl.ds(pl.multiple_of(n * TILE % rec_piece, LANES), TILE)]
+                    products.append(
+                        lax.dot_general(
+                            block, u_fac[:, columns(first_tile + n)], NT_DOT, preferred_element_type=jnp.float32
+                        )
+                    )
+                at = first_tile // 2 + pair
+
+                def store(j, value):
+                    back[j, :, columns(at, LANES)] = masked(value, ranks[2 * at, j], ranks[2 * at + 1, j])
+
+                spread_out(products[0], products[1], back, store)
+                return carry
+
+            lax.fori_loop(0, half // 2, one, 0)
+
+        back_pairs(b_in, side * half)
+        across(b_in.at[k], d_in.at[k], d_sems, k).wait_recv()
+        back_pairs(d_in, partner * half)
+
+        for step in list(range(1, freqs)) + [0]:
+            target = lax.rem(here + step, freqs)
+
+            def one(n, carry):
+                j = target * tiles_each + n
+                value = jnp.dot(back[j], v_fac[:, columns(j)], preferred_element_type=jnp.float32).astype(jnp.bfloat16)
+                if step == 0:
+                    g_in[k, here, :, columns(n)] = value
+                else:
+                    g_out[k, target, :, columns(n)] = value
+                return carry
+
+            lax.fori_loop(0, tiles_each, one, 0)
+            if step > 0:
+                send(along(g_out, g_in, g_sems, k, step))
+
+    def window_src(sweep, c):
+        k = sweep * chunks + c
+        if sweep == 0 and c == 0:
+            loads[4].wait()
+        for step in range(1, freqs):
+            arrived(g_out, g_in, g_sems, k, step)
+        window(k, c, g_in, h_out, h_in, onset_src)
+        for step in range(1, freqs):
+            send(along(h_out, h_in, h_sems, k, step))
+        h_in[k, here] = h_out[k, here]
+
+    def finish(sweep, c):
+        k = sweep * chunks + c
+        rows = slice(c * CHUNK, (c + 1) * CHUNK)
+        for step in range(1, freqs):
+            arrived(h_out, h_in, h_sems, k, step)
+        last = sweep == ITERS - 1
+        base = chunks if last else 0
+        for q in range(freqs):
+            lanes = slice(q * src_piece, (q + 1) * src_piece)
+            start = focus[:, rows, lanes].reshape(2 * CHUNK, src_piece).astype(jnp.float32)
+            plus[base + c, :, lanes] = (start + h_in[k, q].astype(jnp.float32)).astype(jnp.bfloat16)
+        if last:
+            for part in range(2):
+                store = pltpu.make_async_copy(
+                    plus.at[base + c, pl.ds(part * CHUNK, CHUNK), :],
+                    plus_hbm.at[part, pl.ds(c * CHUNK, CHUNK), :],
+                    store_sem.at[0, c, part],
+                )
+                store.start()
+                stores.append(store)
+
+    loads[0].wait()
+    loads[1].wait()
+    stages = [forward, reduce, window_rec, spread, adjoint, window_src, finish]
+    for sweep in range(ITERS):
+        for stage in stages:
+            for c in range(chunks):
+                stage(sweep, c)
+    for copy in sends:
+        copy.wait_send()
+    for store in stores:
+        store.wait()
+
+
+def whole_in_one(axes, focus_direct, u_factors, v_factors, tile_ranks, onset_rec, onset_src):
+    freqs = axes["freq"]
+    points, sources = focus_direct.shape[2:]
+    receivers = u_factors.shape[-1]
+    block = onset_rec.shape[1]
+    rec_piece, src_piece = block // freqs, sources // freqs
+    row_tiles, col_tiles = receivers // TILE, sources // TILE
+    chunks = points // CHUNK
+    runs = ITERS * chunks
+    rows = 2 * CHUNK
+    bf16, f32 = jnp.bfloat16, jnp.float32
+    small = pltpu.VMEM((runs, freqs, rows, rec_piece), bf16)
+    large = pltpu.VMEM((runs, freqs, rows, src_piece), bf16)
+    dma = pltpu.SemaphoreType.DMA
+    anywhere = pl.BlockSpec(memory_space=pl.ANY)
+    plus, minus = pl.pallas_call(
+        functools.partial(kernel, axes),
+        out_shape=(
+            jax.ShapeDtypeStruct((2, points, sources), bf16),
+            jax.ShapeDtypeStruct((2, points, block), bf16),
+        ),
+        in_specs=[anywhere, anywhere, anywhere, pl.BlockSpec(memory_space=pltpu.SMEM), anywhere, anywhere],
+        out_specs=(anywhere, anywhere),
+        scratch_shapes=[
+            pltpu.VMEM((2, points, sources), bf16),
+            pltpu.VMEM((col_tiles * 2 * RANK, receivers), bf16),
+            pltpu.VMEM((row_tiles * 2 * RANK, sources), bf16),
+            pltpu.VMEM((points, rec_piece), jnp.int32),
+            pltpu.VMEM((points, src_piece), jnp.int32),
+            pltpu.VMEM((2 * chunks, rows, sources), bf16),
+            pltpu.VMEM((row_tiles, rows, col_tiles * 2 * RANK), bf16),
+            pltpu.VMEM((col_tiles, rows, row_tiles * 2 * RANK), bf16),
+            pltpu.VMEM((chunks, rows, block), f32),
+            pltpu.VMEM((runs, rows, block), bf16),
+            pltpu.VMEM((runs, rows, block), bf16),
+            small, small, small, small, small,
+            large, large, large, large,
+            dma((5,)),
+            dma((2, chunks, 2 * freqs)),
+            dma((2, runs)),
+            dma((2, runs)),
+            dma((2, runs, freqs - 1)),
+            dma((2, runs, freqs - 1)),
+            dma((2, runs, freqs - 1)),
+            dma((2, runs, freqs - 1)),
+        ],
+        compiler_params=pltpu.CompilerParams(
+            collective_id=0, has_side_effects=True, vmem_limit_bytes=48 * 1024 * 1024
+        ),
+    )(
+        focus_direct[0],
+        u_factors.reshape(col_tiles * 2 * RANK, receivers),
+        v_factors.reshape(row_tiles * 2 * RANK, sources),
+        tile_ranks[0],
+        onset_rec,
+        onset_src,
+    )
+    return plus[None], minus[None]
+
+
+def fits(axes, focus_direct, u_factors, onset_rec):
+    freqs, sides = axes["freq"], axes["src"]
+    points, sources = focus_direct.shape[2:]
+    receivers = u_factors.shape[-1]
+    return (
+        sides == 2
+        and focus_direct.shape[0] == 1
+        and freqs > 1
+        and points % CHUNK == 0
+        and onset_rec.shape[1] % (freqs * TILE) == 0
+        and sources % (freqs * TILE) == 0
+        and receivers % (sides * 2 * TILE) == 0
+    )
+
+
 def solution(mesh):
     placed = (
         P("freq", None, ("groups", "vp"), "src"),
@@ -138,8 +569,16 @@
         P(("groups", "vp"), "src"),
         P(("groups", "vp"), "src"),
     )
+    axes = dict(mesh.shape)
+
+    def part(focus_direct, u_factors, v_factors, tile_ranks, onset_rec, onset_src):
+        args = (focus_direct, u_factors, v_factors, tile_ranks, onset_rec, onset_src)
+        if fits(axes, focus_direct, u_factors, onset_rec):
+            return whole_in_one(axes, *args)
+        return per_device(*args)
+
     return jax.shard_map(
-        per_device,
+        part,
         mesh=mesh,
         in_specs=placed,
         out_specs=(

time: 486 us -> 141 us (0.29); the launches traced: 478 us -> 141 us
  matrix products: 207 us -> 0 us
  Pallas kernels: 0 us -> 135 us
  blocking collectives: 99 us -> 0 us
  local copies, waits for them, and re-layouts: 81.7 us -> 5.43 us
  waiting for transfers between devices: 52 us -> 0 us
  between operations: 15.2 us -> 0.65 us
  starting transfers between devices: 12.6 us -> 0 us
  other arithmetic: 10.8 us -> 0 us
    dot_general x24 -> x0, matrix products: 190 us -> none  [the longest x4 117 us: window(): jnp.einsum('vmt,cft->fcvm', signal, forward, precision=lax.Precision.HIGH...]
    pallas_call x0 -> x1, Pallas kernels: none -> 135 us  [whole_in_one(): pl.pallas_call(functools.partial(kernel, axes), out_shape=(jax.ShapeDtype...]
    all_to_all x5 -> x0, blocking collectives: 86.1 us -> none  [the longest x2 42.2 us: per_device(): lax.all_to_all(src_windowed.astype(jnp.bfloat16), 'freq', split_axis=0, c...]
    unnamed x66 -> x10, local copies, waits for them, and re-layouts: 42.3 us -> 5.43 us
    reduce_scatter x2 -> x0, waiting for transfers between devices: 26.5 us -> none  [per_device(): lax.psum_scatter(partial_terms.astype(jnp.bfloat16), 'src', scatter_dimen...]
    all_to_all x3 -> x0, waiting for transfers between devices: 25.4 us -> none  [the longest x1 17.3 us: per_device(): lax.all_to_all(adjoint.astype(jnp.bfloat16), 'freq', split_axis=3, concat...]
    unnamed x16 -> x0, matrix products: 16.6 us -> none
    all_gather x2 -> x0, blocking collectives: 12.8 us -> none  [per_device(): minus_all = lax.all_gather(minus, 'src', axis=3, tiled=True)]
  transfers between devices with their start and end apart: 5 -> 0, of which waited for: 5 -> 0; matrix products, arithmetic and copies ran while one was open for 1% -> 0% of each run, Pallas kernels for 0% -> 0%
where the time goes in v1:
time: 141 us
  Pallas kernels  135 us (96%)
  local copies, waits for them, and re-layouts  5.43 us (4%)
    pallas_call x1, Pallas kernels, whole_in_one(): pl.pallas_call(functools.partial(kernel, axes), out_shape=(jax.ShapeDtype...  135 us
    unnamed x10, local copies, waits for them, and re-layouts  5.43 us

profile of v1, /device:TPU:0, one launch (start us, length us, event | category | flops | bytes accessed | tf_op | source)
XLA Modules:
  0.0 141.1 jit_solution(5212060067101332046)
XLA Ops:
  0.6 0.0 copy-start
  0.6 1.1 copy-done
  1.8 0.0 copy-start.1
  1.8 1.1 copy-done.1
  2.9 0.0 copy-start.2
  2.9 0.9 copy-done.2
  3.8 0.0 copy-start.3
  3.8 0.7 copy-done.3
  4.5 135.0 %shard_map.77 = (bf16[2,48,4096]{2,1,0:T(8,128)(2,1)S(1)}, bf16[2,48,1024]{2,1,0:T(8,128)(2,1)S(1)}) custom-call(bf16[2,48,4096]{2,1,0:T(8,128)(2,1)S(1)} %bitcast.6, bf16[1024,2048]{1,0:T(8,128)(2,1)} %bitcast.10, bf16[512,4096]{1,0:T(8,128)(2,1)} %bitcast.11, s32[8,16]{1,0:T(8,128)S(1)} %bitcast.9, s32[48,1024]{1,0:T(8,128)S(1)} %copy-done.2, ...), custom_call_target="tpu_custom_call" | custom-call | tf_op jit(solution)/shard_map/pallas_call | solution.py:503
  139.6 0.9 copy.10
  140.4 0.7 copy.11
Async XLA Ops:
  0.6 1.1 copy-start
  1.8 1.1 copy-start.1
  2.9 0.9 copy-start.2
  3.8 0.7 copy-start.3

commit v2 on v1

--- a/solution.py
+++ b/solution.py
@@ -16,6 +16,14 @@
 ITERS = 2
 CHUNK = 16
 LANES = 128
+VMEM_BYTES = 64 * 1024 * 1024 - 512 * 1024
+
+
+ORDER = (
+    0, 1, 100, 2, 101, 200, 102, 300, 201, 202, 400, 301, 401, 500,
+    302, 402, 501, 600, 10, 502, 601, 11, 110, 111, 602, 12, 211, 112,
+    311, 210, 212, 411, 312, 310, 412, 410, 511, 512, 510, 611, 612, 610,
+)
 
 
 def make_tables(count):
@@ -135,6 +143,21 @@
     return (plus, minus)
 
 
+def repeat(count, width, step):
+    width = math.gcd(count, width)
+    if count == width:
+        for n in range(count):
+            step(n)
+        return
+
+    def turn(n, carry):
+        for t in range(width):
+            step(n * width + t)
+        return carry
+
+    lax.fori_loop(0, count // width, turn, 0)
+
+
 def lane_index(rows):
     return lax.broadcasted_iota(jnp.int32, (rows, LANES), 1)
 
@@ -226,8 +249,8 @@
 
 
 def kernel(
-    axes, focus_hbm, u_hbm, v_hbm, ranks, onset_rec_hbm, onset_src_hbm, plus_hbm, minus_hbm,
-    focus, u_fac, v_fac, onset_rec, onset_src, plus, coeff, back, kept,
+    axes, focus_hbm, u_hbm, v_hbm, ranks_hbm, onset_rec_hbm, onset_src_hbm, plus_hbm, minus_hbm,
+    ranks, focus, u_fac, v_fac, onset_rec, onset_src, plus, coeff, back, kept,
     x_out, x_in, a_out, a_in, b_out, b_in, d_in, g_out, g_in, h_out, h_in,
     load_sem, store_sem, x_sems, d_sems, a_sems, b_sems, g_sems, h_sems,
 ):
@@ -246,6 +269,7 @@
 
     loads = [
         pltpu.make_async_copy(focus_hbm, focus, load_sem.at[0]),
+        pltpu.make_async_copy(ranks_hbm, ranks, load_sem.at[5]),
         pltpu.make_async_copy(v_hbm, v_fac, load_sem.at[1]),
         pltpu.make_async_copy(u_hbm, u_fac, load_sem.at[2]),
         pltpu.make_async_copy(
@@ -264,12 +288,13 @@
             barrier, inc=1, device_id={"freq": lax.rem(here + step, freqs)}, device_id_type=pl.DeviceIdType.MESH
         )
     pl.semaphore_signal(barrier, inc=1, device_id={"src": partner}, device_id_type=pl.DeviceIdType.MESH)
-    pl.semaphore_wait(barrier, freqs)
 
     sends = []
     stores = []
 
     def columns(index, size=TILE):
+        if isinstance(index, int):
+            return pl.ds(index * size, size)
         return pl.ds(pl.multiple_of(index * size, size), size)
 
     def across(source, target, sems, k):
@@ -298,7 +323,7 @@
         copy.start()
         sends.append(copy)
 
-    def spread_out(first, second, into, store):
+    def spread_out(first, second, store):
         for q in range(first.shape[1] // LANES):
             lanes = slice(q * LANES, (q + 1) * LANES)
             even, odd = pair_up(combine(first[:, lanes]), combine(second[:, lanes]))
@@ -309,7 +334,7 @@
         k = sweep * chunks + c
         rows = slice(c * CHUNK, (c + 1) * CHUNK)
 
-        def one(pair, carry):
+        def one(pair):
             products = []
             for t in range(2):
                 cols = columns(2 * pair + t)
@@ -322,27 +347,28 @@
             def store(i, value):
                 coeff[i, :, columns(pair, LANES)] = masked(value, ranks[i, 2 * pair], ranks[i, 2 * pair + 1])
 
-            spread_out(products[0], products[1], coeff, store)
-            return carry
-
-        lax.fori_loop(0, col_tiles // 2, one, 0)
+            spread_out(products[0], products[1], store)
+
+        repeat(col_tiles // 2, 2, one)
         if sweep == 0 and c == 0:
-            loads[2].wait()
+            loads[3].wait()
 
         def product(i):
             return jnp.dot(coeff[i], u_fac[:, columns(i)], preferred_element_type=jnp.float32)
 
-        def theirs(n, carry):
+        def theirs(n):
             x_out[k, :, columns(n)] = product(partner * half + n).astype(jnp.bfloat16)
-            return carry
-
-        def ours(n, carry):
+
+        def ours(n):
             kept[c, :, columns(n)] = product(side * half + n)
-            return carry
-
-        lax.fori_loop(0, half, theirs, 0)
+
+        for n in range(half):
+            theirs(n)
+        if sweep == 0 and c == 0:
+            pl.semaphore_wait(barrier, freqs)
         send(across(x_out.at[k], x_in.at[k], x_sems, k))
-        lax.fori_loop(0, half, ours, 0)
+        for n in range(half):
+            ours(n)
 
     def reduce(sweep, c):
         k = sweep * chunks + c
@@ -357,7 +383,7 @@
     def window(k, c, from_ref, to_ref, own_ref, onset):
         rows = slice(c * CHUNK, (c + 1) * CHUNK)
 
-        def one(n, carry):
+        def one(n):
             lanes = columns(n, LANES)
             spectra = []
             for f in range(freqs):
@@ -365,14 +391,13 @@
                 spectra.append((both[:CHUNK], both[CHUNK:]))
             for f, (real, imag) in enumerate(window_block(spectra, onset[rows, lanes], freqs)):
                 to_ref[k, f, :, lanes] = jnp.concatenate([real, imag], axis=0).astype(jnp.bfloat16)
-            return carry
-
-        lax.fori_loop(0, onset.shape[1] // LANES, one, 0)
+
+        repeat(onset.shape[1] // LANES, 2, one)
 
     def window_rec(sweep, c):
         k = sweep * chunks + c
         if sweep == 0 and c == 0:
-            loads[3].wait()
+            loads[4].wait()
         for step in range(1, freqs):
             arrived(a_out, a_in, a_sems, k, step)
         window(k, c, a_in, b_out, b_in, onset_rec)
@@ -400,7 +425,7 @@
         k = sweep * chunks + c
 
         def back_pairs(source, first_tile):
-            def one(pair, carry):
+            def one(pair):
                 products = []
                 for t in range(2):
                     n = 2 * pair + t
@@ -415,10 +440,9 @@
                 def store(j, value):
                     back[j, :, columns(at, LANES)] = masked(value, ranks[2 * at, j], ranks[2 * at + 1, j])
 
-                spread_out(products[0], products[1], back, store)
-                return carry
-
-            lax.fori_loop(0, half // 2, one, 0)
+                spread_out(products[0], products[1], store)
+
+            repeat(half // 2, 2, one)
 
         back_pairs(b_in, side * half)
         across(b_in.at[k], d_in.at[k], d_sems, k).wait_recv()
@@ -427,23 +451,22 @@
         for step in list(range(1, freqs)) + [0]:
             target = lax.rem(here + step, freqs)
 
-            def one(n, carry):
+            def one(n):
                 j = target * tiles_each + n
                 value = jnp.dot(back[j], v_fac[:, columns(j)], preferred_element_type=jnp.float32).astype(jnp.bfloat16)
                 if step == 0:
                     g_in[k, here, :, columns(n)] = value
                 else:
                     g_out[k, target, :, columns(n)] = value
-                return carry
-
-            lax.fori_loop(0, tiles_each, one, 0)
+
+            repeat(tiles_each, 4, one)
             if step > 0:
                 send(along(g_out, g_in, g_sems, k, step))
 
     def window_src(sweep, c):
         k = sweep * chunks + c
         if sweep == 0 and c == 0:
-            loads[4].wait()
+            loads[5].wait()
         for step in range(1, freqs):
             arrived(g_out, g_in, g_sems, k, step)
         window(k, c, g_in, h_out, h_in, onset_src)
@@ -472,17 +495,21 @@
                 store.start()
                 stores.append(store)
 
-    loads[0].wait()
-    loads[1].wait()
+    for load in loads[:3]:
+        load.wait()
     stages = [forward, reduce, window_rec, spread, adjoint, window_src, finish]
-    for sweep in range(ITERS):
-        for stage in stages:
-            for c in range(chunks):
-                stage(sweep, c)
+    for stage, sweep, c in order_of(chunks):
+        stages[stage](sweep, c)
     for copy in sends:
         copy.wait_send()
     for store in stores:
         store.wait()
+
+
+def order_of(chunks):
+    if chunks == 3:
+        return [(code // 100, code // 10 % 10, code % 10) for code in ORDER]
+    return [(stage, sweep, c) for sweep in range(ITERS) for stage in range(7) for c in range(chunks)]
 
 
 def whole_in_one(axes, focus_direct, u_factors, v_factors, tile_ranks, onset_rec, onset_src):
@@ -506,9 +533,10 @@
             jax.ShapeDtypeStruct((2, points, sources), bf16),
             jax.ShapeDtypeStruct((2, points, block), bf16),
         ),
-        in_specs=[anywhere, anywhere, anywhere, pl.BlockSpec(memory_space=pltpu.SMEM), anywhere, anywhere],
+        in_specs=[anywhere] * 6,
         out_specs=(anywhere, anywhere),
         scratch_shapes=[
+            pltpu.SMEM((row_tiles, col_tiles), jnp.int32),
             pltpu.VMEM((2, points, sources), bf16),
             pltpu.VMEM((col_tiles * 2 * RANK, receivers), bf16),
             pltpu.VMEM((row_tiles * 2 * RANK, sources), bf16),
@@ -522,7 +550,7 @@
             pltpu.VMEM((runs, rows, block), bf16),
             small, small, small, small, small,
             large, large, large, large,
-            dma((5,)),
+            dma((6,)),
             dma((2, chunks, 2 * freqs)),
             dma((2, runs)),
             dma((2, runs)),
@@ -532,7 +560,7 @@
             dma((2, runs, freqs - 1)),
         ],
         compiler_params=pltpu.CompilerParams(
-            collective_id=0, has_side_effects=True, vmem_limit_bytes=48 * 1024 * 1024
+            collective_id=0, has_side_effects=True, vmem_limit_bytes=VMEM_BYTES
         ),
     )(
         focus_direct[0],

time: 141 us -> 115 us (0.82)
  Pallas kernels: 135 us -> 110 us
  local copies, waits for them, and re-layouts: 5.43 us -> 3.68 us
    pallas_call x1, Pallas kernels: 135 us -> 110 us  [whole_in_one(): pl.pallas_call(functools.partial(kernel, axes), out_shape=(jax.ShapeDtype...]
    unnamed x10 -> x2, local copies, waits for them, and re-layouts: 5.43 us -> 3.68 us
where the time goes in v2:
time: 115 us
  Pallas kernels  110 us (96%)
  local copies, waits for them, and re-layouts  3.68 us (3%)
    pallas_call x1, Pallas kernels, whole_in_one(): pl.pallas_call(functools.partial(kernel, axes), out_shape=(jax.ShapeDtype...  110 us
    unnamed x2, local copies, waits for them, and re-layouts  3.68 us

profile of v2, /device:TPU:0, one launch (start us, length us, event | category | flops | bytes accessed | tf_op | source)
XLA Modules:
  0.0 114.7 jit_solution(15020762718783965517)
XLA Ops:
  0.6 110.4 %shard_map.77 = (bf16[2,48,4096]{2,1,0:T(8,128)(2,1)}, bf16[2,48,1024]{2,1,0:T(8,128)(2,1)}) custom-call(bf16[2,48,4096]{2,1,0:T(8,128)(2,1)} %bitcast.8, bf16[1024,2048]{1,0:T(8,128)(2,1)} %bitcast.6, bf16[512,4096]{1,0:T(8,128)(2,1)} %bitcast.7, s32[8,16]{1,0:T(8,128)} %bitcast.11, s32[48,1024]{1,0:T(8,128)} %onset_rec_hbm.1, s32[48,4096]{1,0:T(8,128)} %onset_src_hbm.1), custom_call_target="tpu_custom_call" | custom-call | tf_op jit(solution)/shard_map/pallas_call | solution.py:530
  111.0 2.1 %copy.10 = bf16[1,2,48,4096]{3,2,1,0:T(8,128)(2,1)} copy(bf16[1,2,48,4096]{3,2,1,0:T(8,128)(2,1)} %bitcast.9) | data formatting | bytes 1572864
  113.1 1.6 %copy.11 = bf16[1,2,48,1024]{3,2,1,0:T(8,128)(2,1)} copy(bf16[1,2,48,1024]{3,2,1,0:T(8,128)(2,1)} %bitcast.10) | data formatting | bytes 393216

commit v3 on v2

--- a/solution.py
+++ b/solution.py
@@ -16,13 +16,15 @@
 ITERS = 2
 CHUNK = 16
 LANES = 128
-VMEM_BYTES = 64 * 1024 * 1024 - 512 * 1024
+VMEM_BYTES = 48 * 1024 * 1024
 
 
 ORDER = (
-    0, 1, 100, 2, 101, 200, 102, 300, 201, 202, 400, 301, 401, 500,
-    302, 402, 501, 600, 10, 502, 601, 11, 110, 111, 602, 12, 211, 112,
-    311, 210, 212, 411, 312, 310, 412, 410, 511, 512, 510, 611, 612, 610,
+    1, 0, 100, 200, 2, 102, 300, 202, 101, 400, 302, 201, 500, 301,
+    402, 600, 502, 401, 602, 700, 501, 702, 802, 800, 10, 601, 12, 112,
+    110, 210, 212, 310, 312, 410, 701, 412, 510, 801, 610, 512, 11, 612,
+    710, 111, 211, 311, 712, 411, 812, 810, 22, 511, 20, 611, 711, 122,
+    811, 21, 120, 121,
 )
 
 
@@ -266,6 +268,9 @@
     rec_piece = onset_rec.shape[1]
     src_piece = onset_src.shape[1]
     tiles_each = src_piece // TILE
+    src_half = src_piece // 2
+    tiles_half = tiles_each // 2
+    pairs_half = tiles_half // 2
 
     loads = [
         pltpu.make_async_copy(focus_hbm, focus, load_sem.at[0]),
@@ -292,6 +297,17 @@
     sends = []
     stores = []
 
+    waited = set()
+
+    def need(n):
+        if n in waited:
+            return
+        waited.add(n)
+        if n < len(loads):
+            loads[n].wait()
+        else:
+            pl.semaphore_wait(barrier, freqs)
+
     def columns(index, size=TILE):
         if isinstance(index, int):
             return pl.ds(index * size, size)
@@ -330,45 +346,57 @@
             store(2 * q, even)
             store(2 * q + 1, odd)
 
+    def collect(sweep, c, part):
+        rows = slice(c * CHUNK, (c + 1) * CHUNK)
+        if sweep > 0:
+            k = 2 * ((sweep - 1) * chunks + c) + part
+            for step in range(1, freqs):
+                arrived(h_out, h_in, h_sems, k, step)
+            for q in range(freqs):
+                lanes = pl.ds(q * src_piece + part * src_half, src_half)
+                start = focus[:, rows, lanes].reshape(2 * CHUNK, src_half).astype(jnp.float32)
+                plus[(sweep - 1) * chunks + c, :, lanes] = (start + h_in[k, q].astype(jnp.float32)).astype(jnp.bfloat16)
+        if sweep == ITERS:
+            if part == 1:
+                for side_of in range(2):
+                    store = pltpu.make_async_copy(
+                        plus.at[(sweep - 1) * chunks + c, pl.ds(side_of * CHUNK, CHUNK), :],
+                        plus_hbm.at[side_of, pl.ds(c * CHUNK, CHUNK), :],
+                        store_sem.at[0, c, side_of],
+                    )
+                    store.start()
+                    stores.append(store)
+            return
+        for q in range(freqs):
+            for n in range(pairs_half):
+                pair = (q * src_piece + part * src_half) // (2 * TILE) + n
+                products = []
+                for t in range(2):
+                    cols = columns(2 * pair + t)
+                    if sweep == 0:
+                        block = focus[:, rows, cols].reshape(2 * CHUNK, TILE)
+                    else:
+                        block = plus[(sweep - 1) * chunks + c, :, cols]
+                    products.append(lax.dot_general(block, v_fac[:, cols], NT_DOT, preferred_element_type=jnp.float32))
+
+                def store(i, value):
+                    coeff[c, i, :, columns(pair, LANES)] = masked(value, ranks[i, 2 * pair], ranks[i, 2 * pair + 1])
+
+                spread_out(products[0], products[1], store)
+
     def forward(sweep, c):
         k = sweep * chunks + c
-        rows = slice(c * CHUNK, (c + 1) * CHUNK)
-
-        def one(pair):
-            products = []
-            for t in range(2):
-                cols = columns(2 * pair + t)
-                if sweep == 0:
-                    block = focus[:, rows, cols].reshape(2 * CHUNK, TILE)
-                else:
-                    block = plus[c, :, cols]
-                products.append(lax.dot_general(block, v_fac[:, cols], NT_DOT, preferred_element_type=jnp.float32))
-
-            def store(i, value):
-                coeff[i, :, columns(pair, LANES)] = masked(value, ranks[i, 2 * pair], ranks[i, 2 * pair + 1])
-
-            spread_out(products[0], products[1], store)
-
-        repeat(col_tiles // 2, 2, one)
-        if sweep == 0 and c == 0:
-            loads[3].wait()
+        need(3)
 
         def product(i):
-            return jnp.dot(coeff[i], u_fac[:, columns(i)], preferred_element_type=jnp.float32)
-
-        def theirs(n):
+            return jnp.dot(coeff[c, i], u_fac[:, columns(i)], preferred_element_type=jnp.float32)
+
+        for n in range(half):
             x_out[k, :, columns(n)] = product(partner * half + n).astype(jnp.bfloat16)
-
-        def ours(n):
-            kept[c, :, columns(n)] = product(side * half + n)
-
-        for n in range(half):
-            theirs(n)
-        if sweep == 0 and c == 0:
-            pl.semaphore_wait(barrier, freqs)
+        need(6)
         send(across(x_out.at[k], x_in.at[k], x_sems, k))
         for n in range(half):
-            ours(n)
+            kept[c, :, columns(n)] = product(side * half + n)
 
     def reduce(sweep, c):
         k = sweep * chunks + c
@@ -380,7 +408,7 @@
             send(along(a_out, a_in, a_sems, k, step))
         a_in[k, here] = a_out[k, here]
 
-    def window(k, c, from_ref, to_ref, own_ref, onset):
+    def window(k, c, from_ref, to_ref, onset, first, size):
         rows = slice(c * CHUNK, (c + 1) * CHUNK)
 
         def one(n):
@@ -389,18 +417,17 @@
             for f in range(freqs):
                 both = from_ref[k, f, :, lanes].astype(jnp.float32)
                 spectra.append((both[:CHUNK], both[CHUNK:]))
-            for f, (real, imag) in enumerate(window_block(spectra, onset[rows, lanes], freqs)):
+            for f, (real, imag) in enumerate(window_block(spectra, onset[rows, columns(n + first // LANES, LANES)], freqs)):
                 to_ref[k, f, :, lanes] = jnp.concatenate([real, imag], axis=0).astype(jnp.bfloat16)
 
-        repeat(onset.shape[1] // LANES, 2, one)
+        repeat(size // LANES, 2, one)
 
     def window_rec(sweep, c):
         k = sweep * chunks + c
-        if sweep == 0 and c == 0:
-            loads[4].wait()
+        need(4)
         for step in range(1, freqs):
             arrived(a_out, a_in, a_sems, k, step)
-        window(k, c, a_in, b_out, b_in, onset_rec)
+        window(k, c, a_in, b_out, onset_rec, 0, rec_piece)
         for step in range(1, freqs):
             send(along(b_out, b_in, b_sems, k, step))
         b_in[k, here] = b_out[k, here]
@@ -448,56 +475,36 @@
         across(b_in.at[k], d_in.at[k], d_sems, k).wait_recv()
         back_pairs(d_in, partner * half)
 
-        for step in list(range(1, freqs)) + [0]:
-            target = lax.rem(here + step, freqs)
-
-            def one(n):
-                j = target * tiles_each + n
-                value = jnp.dot(back[j], v_fac[:, columns(j)], preferred_element_type=jnp.float32).astype(jnp.bfloat16)
-                if step == 0:
-                    g_in[k, here, :, columns(n)] = value
-                else:
-                    g_out[k, target, :, columns(n)] = value
-
-            repeat(tiles_each, 4, one)
-            if step > 0:
-                send(along(g_out, g_in, g_sems, k, step))
-
-    def window_src(sweep, c):
-        k = sweep * chunks + c
-        if sweep == 0 and c == 0:
-            loads[5].wait()
+        for part in range(2):
+            for step in list(range(1, freqs)) + [0]:
+                target = lax.rem(here + step, freqs)
+                for n in range(tiles_half):
+                    j = target * tiles_each + part * tiles_half + n
+                    value = jnp.dot(back[j], v_fac[:, columns(j)], preferred_element_type=jnp.float32)
+                    value = value.astype(jnp.bfloat16)
+                    if step == 0:
+                        g_in[2 * k + part, here, :, columns(n)] = value
+                    else:
+                        g_out[2 * k + part, target, :, columns(n)] = value
+                if step > 0:
+                    send(along(g_out, g_in, g_sems, 2 * k + part, step))
+
+    def window_src(sweep, c, part):
+        k = 2 * (sweep * chunks + c) + part
+        need(5)
         for step in range(1, freqs):
             arrived(g_out, g_in, g_sems, k, step)
-        window(k, c, g_in, h_out, h_in, onset_src)
+        window(k, c, g_in, h_out, onset_src, part * src_half, src_half)
         for step in range(1, freqs):
             send(along(h_out, h_in, h_sems, k, step))
         h_in[k, here] = h_out[k, here]
 
-    def finish(sweep, c):
-        k = sweep * chunks + c
-        rows = slice(c * CHUNK, (c + 1) * CHUNK)
-        for step in range(1, freqs):
-            arrived(h_out, h_in, h_sems, k, step)
-        last = sweep == ITERS - 1
-        base = chunks if last else 0
-        for q in range(freqs):
-            lanes = slice(q * src_piece, (q + 1) * src_piece)
-            start = focus[:, rows, lanes].reshape(2 * CHUNK, src_piece).astype(jnp.float32)
-            plus[base + c, :, lanes] = (start + h_in[k, q].astype(jnp.float32)).astype(jnp.bfloat16)
-        if last:
-            for part in range(2):
-                store = pltpu.make_async_copy(
-                    plus.at[base + c, pl.ds(part * CHUNK, CHUNK), :],
-                    plus_hbm.at[part, pl.ds(c * CHUNK, CHUNK), :],
-                    store_sem.at[0, c, part],
-                )
-                store.start()
-                stores.append(store)
-
-    for load in loads[:3]:
-        load.wait()
-    stages = [forward, reduce, window_rec, spread, adjoint, window_src, finish]
+    for n in range(3):
+        need(n)
+    stages = [
+        functools.partial(collect, part=0), functools.partial(collect, part=1), forward, reduce, window_rec, spread,
+        adjoint, functools.partial(window_src, part=0), functools.partial(window_src, part=1),
+    ]
     for stage, sweep, c in order_of(chunks):
         stages[stage](sweep, c)
     for copy in sends:
@@ -509,7 +516,8 @@
 def order_of(chunks):
     if chunks == 3:
         return [(code // 100, code // 10 % 10, code % 10) for code in ORDER]
-    return [(stage, sweep, c) for sweep in range(ITERS) for stage in range(7) for c in range(chunks)]
+    whole = [(stage, sweep, c) for sweep in range(ITERS) for stage in range(9) for c in range(chunks)]
+    return whole + [(stage, ITERS, c) for stage in range(2) for c in range(chunks)]
 
 
 def whole_in_one(axes, focus_direct, u_factors, v_factors, tile_ranks, onset_rec, onset_src):
@@ -524,7 +532,7 @@
     rows = 2 * CHUNK
     bf16, f32 = jnp.bfloat16, jnp.float32
     small = pltpu.VMEM((runs, freqs, rows, rec_piece), bf16)
-    large = pltpu.VMEM((runs, freqs, rows, src_piece), bf16)
+    large = pltpu.VMEM((2 * runs, freqs, rows, src_piece // 2), bf16)
     dma = pltpu.SemaphoreType.DMA
     anywhere = pl.BlockSpec(memory_space=pl.ANY)
     plus, minus = pl.pallas_call(
@@ -533,7 +541,7 @@
             jax.ShapeDtypeStruct((2, points, sources), bf16),
             jax.ShapeDtypeStruct((2, points, block), bf16),
         ),
-        in_specs=[anywhere] * 6,
+        in_specs=[pl.BlockSpec(memory_space=pltpu.HBM)] * 6,
         out_specs=(anywhere, anywhere),
         scratch_shapes=[
             pltpu.SMEM((row_tiles, col_tiles), jnp.int32),
@@ -543,7 +551,7 @@
             pltpu.VMEM((points, rec_piece), jnp.int32),
             pltpu.VMEM((points, src_piece), jnp.int32),
             pltpu.VMEM((2 * chunks, rows, sources), bf16),
-            pltpu.VMEM((row_tiles, rows, col_tiles * 2 * RANK), bf16),
+            pltpu.VMEM((chunks, row_tiles, rows, col_tiles * 2 * RANK), bf16),
             pltpu.VMEM((col_tiles, rows, row_tiles * 2 * RANK), bf16),
             pltpu.VMEM((chunks, rows, block), f32),
             pltpu.VMEM((runs, rows, block), bf16),
@@ -556,8 +564,8 @@
             dma((2, runs)),
             dma((2, runs, freqs - 1)),
             dma((2, runs, freqs - 1)),
-            dma((2, runs, freqs - 1)),
-            dma((2, runs, freqs - 1)),
+            dma((2, 2 * runs, freqs - 1)),
+            dma((2, 2 * runs, freqs - 1)),
         ],
         compiler_params=pltpu.CompilerParams(
             collective_id=0, has_side_effects=True, vmem_limit_bytes=VMEM_BYTES
@@ -583,7 +591,7 @@
         and freqs > 1
         and points % CHUNK == 0
         and onset_rec.shape[1] % (freqs * TILE) == 0
-        and sources % (freqs * TILE) == 0
+        and sources % (freqs * 4 * TILE) == 0
         and receivers % (sides * 2 * TILE) == 0
     )
 

time: 115 us -> 118 us (1.026)
  Pallas kernels: 110 us -> 112 us
  local copies, waits for them, and re-layouts: 3.68 us -> 5.43 us
    unnamed x2 -> x10, local copies, waits for them, and re-layouts: 3.68 us -> 5.43 us
    pallas_call x1, Pallas kernels: 110 us -> 112 us  [whole_in_one(): pl.pallas_call(functools.partial(kernel, axes), out_shape=(jax.ShapeDtype...]
where the time goes in v3:
time: 118 us
  Pallas kernels  112 us (95%)
  local copies, waits for them, and re-layouts  5.43 us (5%)
    pallas_call x1, Pallas kernels, whole_in_one(): pl.pallas_call(functools.partial(kernel, axes), out_shape=(jax.ShapeDtype...  112 us
    unnamed x10, local copies, waits for them, and re-layouts  5.43 us

profile of v3, /device:TPU:0, one launch (start us, length us, event | category | flops | bytes accessed | tf_op | source)
XLA Modules:
  0.0 117.7 jit_solution(6319070894044032072)
XLA Ops:
  0.6 0.0 copy-start
  0.6 1.1 copy-done
  1.8 0.0 copy-start.1
  1.8 1.1 copy-done.1
  2.9 0.0 copy-start.2
  2.9 0.9 copy-done.2
  3.8 0.0 copy-start.3
  3.8 0.7 copy-done.3
  4.5 111.6 %shard_map.77 = (bf16[2,48,4096]{2,1,0:T(8,128)(2,1)S(1)}, bf16[2,48,1024]{2,1,0:T(8,128)(2,1)S(1)}) custom-call(bf16[2,48,4096]{2,1,0:T(8,128)(2,1)S(1)} %bitcast.6, bf16[1024,2048]{1,0:T(8,128)(2,1)} %bitcast.10, bf16[512,4096]{1,0:T(8,128)(2,1)} %bitcast.11, s32[8,16]{1,0:T(8,128)S(1)} %bitcast.9, s32[48,1024]{1,0:T(8,128)S(1)} %copy-done.2, ...), custom_call_target="tpu_custom_call" | custom-call | tf_op jit(solution)/shard_map/pallas_call | solution.py:538
  116.1 0.9 copy.10
  117.0 0.7 copy.11
Async XLA Ops:
  0.6 1.1 copy-start
  1.8 1.1 copy-start.1
  2.9 0.9 copy-start.2
  3.8 0.7 copy-start.3
